TPU v7x, 32 devices: a whole 2x2x4 slice. The times are simulated.
32 devices in a mesh: coil: 8 (over z, x), frame: 4 (over y, core).
Axes of the slice: x: 2, y: 2, z: 4, core: 2. Of those that a mesh axis runs over, the one named last changes fastest.
Arguments:
- kspace: bfloat16 [32, 1024, 8, 256], P('coil', 'frame'), may hold values from -6 to 6
- sampled_lines: int32 [1024, 8], P('frame'), may hold values from 0 to 63, all different within a row
- sensitivity: float32 [32, 2, 8192], P('coil'), may hold values from -55 to 55
- dictionary: bfloat16 [16384, 2048], P('coil'), may hold values from -55 to 55
- atom_params: float32 [6, 16384], P(None, 'coil'), may hold values from -4 to 4
- concentration: float32 [8192], P('frame'), may hold values from 20 to 3000
Outputs:
- estimates: float32 [6, 8192], P(None, 'frame')
Inputs may be any that keep to these rules, and one draw needn't show every extreme that they name: `sampled_lines`: each frame names 8 different lines.
All inputs are finite; a program needn't handle non-finite values.
Results may differ from a plain program's by a relative error of at most 0.0025.
The roundings to bfloat16 on the way count: a program that leaves them out, or rounds other values in their place, can miss the bound.
Values may be sent and summed in bfloat16 or wider, within the bound.
A program may use at most 192 MiB of HBM per device.

v0:
```python
import math

import jax
import jax.numpy as jnp
from jax import lax
from jax.sharding import PartitionSpec as P

NPE = 64
NRO = 128
ROWS = 64


def readout_table(length):
    position = jnp.arange(length, dtype=jnp.int32)
    angles = (position[:, None] * position[None, :] % length).astype(jnp.float32) * (
        2.0 * math.pi / length
    )
    cos_table = jnp.cos(angles)
    sine_table = jnp.sin(angles)
    upper_half = jnp.concatenate([cos_table, sine_table], axis=1)
    lower_half = jnp.concatenate([-sine_table, cos_table], axis=1)
    return jnp.concatenate([upper_half, lower_half], axis=0).astype(jnp.bfloat16)


def line_phases(line_index, row_count, length):
    row_index = jnp.arange(row_count, dtype=jnp.int32)
    angles = (line_index[:, :, None] * row_index[None, None, :] % length).astype(jnp.float32) * (
        2.0 * math.pi / length
    )
    return (jnp.cos(angles), jnp.sin(angles))


def coil_images(samples, cos_lines, sine_lines, table):
    spread = jnp.dot(samples, table, preferred_element_type=jnp.float32)
    half_width = spread.shape[-1] // 2
    real_part = spread[..., :half_width]
    imag_part = spread[..., half_width:]
    highest = lax.Precision.HIGHEST
    image_re = jnp.einsum("fly,cflx->cfyx", cos_lines, real_part, precision=highest) - jnp.einsum(
        "fly,cflx->cfyx", sine_lines, imag_part, precision=highest
    )
    image_im = jnp.einsum("fly,cflx->cfyx", sine_lines, real_part, precision=highest) + jnp.einsum(
        "fly,cflx->cfyx", cos_lines, imag_part, precision=highest
    )
    return (image_re, image_im)


def combine(image_re, image_im, sensitivity):
    coil_count, frame_count, row_count, column_count = image_re.shape
    flat_re = image_re.reshape(coil_count, frame_count, row_count * column_count)
    flat_im = image_im.reshape(coil_count, frame_count, row_count * column_count)
    sens_re = sensitivity[:, 0][:, None, :]
    sens_im = sensitivity[:, 1][:, None, :]
    part_re = jnp.sum(sens_re * flat_re + sens_im * flat_im, axis=0)
    part_im = jnp.sum(sens_re * flat_im - sens_im * flat_re, axis=0)
    return jnp.stack([part_re, part_im], axis=1)


def atom_scales(dictionary):
    widened = dictionary.astype(jnp.float32)
    return lax.rsqrt(jnp.mean(widened * widened, axis=1) + 1e-06)


def match_stats(dictionary, atom_scale, atom_params, segment, local_kappa):
    frame_count = segment.shape[0]
    voxel_count = segment.shape[-1]
    direct = segment.reshape(2 * frame_count, voxel_count)
    turned = jnp.stack([segment[:, 1], -segment[:, 0]], axis=1).reshape(
        2 * frame_count, voxel_count
    )
    stacked = jnp.concatenate([direct, turned], axis=1)
    inner = jnp.dot(dictionary, stacked, preferred_element_type=jnp.float32)
    magnitude = jnp.sqrt(
        inner[:, :voxel_count] * inner[:, :voxel_count]
        + inner[:, voxel_count:] * inner[:, voxel_count:]
    )
    widened = direct.astype(jnp.float32)
    voxel_scale = lax.rsqrt(jnp.mean(widened * widened, axis=0) + 1e-06)
    logits = (
        magnitude * atom_scale[:, None] * (voxel_scale * local_kappa / (2.0 * frame_count))[None, :]
    )
    peak_score = jnp.max(logits, axis=0)
    weights = jnp.exp(logits - peak_score[None, :])
    total_weight = jnp.sum(weights, axis=0)
    moments = jnp.dot(
        atom_params, weights, precision=lax.Precision.HIGHEST, preferred_element_type=jnp.float32
    )
    return (peak_score, total_weight, moments)


def body(kspace, sampled_lines, sensitivity, dictionary, atom_params, concentration):
    table = readout_table(NRO)
    frame_groups = lax.axis_size("frame")
    coil_groups = lax.axis_size("coil")
    voxel_total = sensitivity.shape[2]
    block_size = voxel_total // frame_groups
    atom_scale = atom_scales(dictionary)
    every_coil = lax.all_to_all(kspace, "coil", split_axis=1, concat_axis=0, tiled=True)
    few_frames = every_coil.shape[1]
    lines_here = lax.dynamic_slice_in_dim(
        sampled_lines, lax.axis_index("coil") * few_frames, few_frames, 0
    )
    cos_sub, sine_sub = line_phases(lines_here, ROWS, NPE)
    all_sens = lax.all_gather(sensitivity, "coil", axis=0, tiled=True)
    image_re, image_im = coil_images(every_coil, cos_sub, sine_sub, table)
    local_sum = combine(image_re, image_im, all_sens).astype(jnp.bfloat16)
    share_size = block_size // coil_groups
    grouped = local_sum.reshape(few_frames, 2, frame_groups, coil_groups, share_size)
    routed = lax.all_to_all(
        lax.all_to_all(grouped, "coil", split_axis=3, concat_axis=0, tiled=True),
        "frame",
        split_axis=2,
        concat_axis=0,
        tiled=True,
    )
    routed = routed.reshape(routed.shape[0], 2, 1, share_size)
    peak_score, total_weight, moments = match_stats(
        dictionary,
        atom_scale,
        atom_params,
        lax.all_gather(routed, "coil", axis=3, tiled=True)[:, :, 0, :],
        concentration,
    )
    statistics = jnp.concatenate([peak_score[None], total_weight[None], moments], axis=0)
    peak_score = statistics[0]
    total_weight = statistics[1]
    moments = statistics[2:]
    peak_global = lax.pmax(peak_score, "coil")
    factor = jnp.exp(peak_score - peak_global)
    total_weight, moments = lax.psum((total_weight * factor, moments * factor[None, :]), "coil")
    return moments / total_weight[None, :]


def solution(mesh):
    in_specs = (
        P("coil", "frame", None, None),
        P("frame", None),
        P("coil", None, None),
        P("coil", None),
        P(None, "coil"),
        P("frame"),
    )
    out_specs = P(None, "frame")
    return jax.shard_map(body, mesh=mesh, in_specs=in_specs, out_specs=out_specs, check_vma=False)
```

profile of v0, /device:TPU:0, one launch (start us, length us, event | category | flops | bytes accessed | tf_op | source)
XLA Modules:
  0.0 680.8 jit_solution(5904640736825295765)
XLA Ops:
  11.3 7.3 %all-to-all-start = ((bf16[4,256,8,256]{3,2,0,1:T(8,128)(2,1)}), bf16[4,256,8,256]{3,2,0,1:T(8,128)(2,1)}, u32[]{:S(2)}, u32[]{:S(2)}) async-start(bf16[4,256,8,256]{3,2,0,1:T(8,128)(2,1)} %copy.30), calls=%async_computation | async-start | bytes 8388608 | tf_op jit(solution)/shard_map/all_to_all | solution.py:98
  20.1 104.6 %all-gather.3.cloned.1.call-done = f32[32,2,8192]{2,1,0:T(2,128)} async-done(((f32[4,2,8192]{2,1,0:T(2,128)}), f32[32,2,8192]{2,1,0:T(2,128)}) %all-gather.3.cloned.1.call-update) | async-done | bytes 2097168 | tf_op jit(solution)/shard_map/all_gather | solution.py:104
  129.2 8.0 %all-to-all-done = bf16[4,256,8,256]{3,2,0,1:T(8,128)(2,1)} async-done(((bf16[4,256,8,256]{3,2,0,1:T(8,128)(2,1)}), bf16[4,256,8,256]{3,2,0,1:T(8,128)(2,1)}, u32[]{:S(2)}, u32[]{:S(2)}) %all-to-all-start) | async-done | bytes 4194336 | tf_op jit(solution)/shard_map/all_to_all | solution.py:98
  137.2 5.9 copy.31
  145.0 31.0 %fusion.14 = f32[32,32,128,64]{2,3,1,0:T(8,128)} fusion(f32[32,32,8,128]{3,1,2,0:T(8,128)S(1)} %get-tuple-element.15, s32[32,8]{1,0:T(8,128)S(1)} %copy.32), kind=kOutput, calls=%fused_computation.26 | convolution fusion | flops 805535744 | bytes 37749760 | tf_op jit(solution)/shard_map/fly,cflx->cfyx/dot_general | solution.py:42
  176.1 31.1 %fusion.16 = f32[32,32,128,64]{2,3,1,0:T(8,128)} fusion(f32[32,32,8,128]{3,1,2,0:T(8,128)S(1)} %get-tuple-element.15, s32[32,8]{1,0:T(8,128)S(1)} %copy.32), kind=kOutput, calls=%fused_computation.28 | convolution fusion | flops 805535744 | bytes 37749760 | tf_op jit(solution)/shard_map/fly,cflx->cfyx/dot_general | solution.py:39
  207.2 31.2 %fusion.20 = f32[32,32,128,64]{2,3,1,0:T(8,128)} fusion(f32[32,32,8,128]{3,1,2,0:T(8,128)S(1)} %get-tuple-element.16, s32[32,8]{1,0:T(8,128)S(1)} %copy.32), kind=kOutput, calls=%fused_computation.32 | convolution fusion | flops 805535744 | bytes 37749760 | tf_op jit(solution)/shard_map/fly,cflx->cfyx/dot_general | solution.py:39
  238.4 49.5 %fusion.1 = (bf16[32,64,128]{2,1,0:T(8,128)(2,1)S(1)}, bf16[32,64,128]{2,1,0:T(8,128)(2,1)S(1)}) fusion(f32[32,64,128]{2,1,0:T(8,128)S(1)} %bitcast.72, f32[32,64,128]{2,1,0:T(8,128)S(1)} %bitcast.71, f32[32,32,128,64]{2,3,1,0:T(8,128)} %fusion.14, f32[32,32,128,64]{2,3,1,0:T(8,128)} %fusion.20, f32[32,32,128,64]{2,3,1,0:T(8,128)} %fusion.16, ...), kind=kOutput, calls=%fused_computation.3 | convolution fusion | flops 888897536 | bytes 108004352 | tf_op jit(solution)/shard_map/fly,cflx->cfyx/dot_general | solution.py:42
  288.9 29.3 %all_to_all.51 = bf16[32,2,4,8,256]{4,2,0,1,3:T(4,128)(2,1)S(1)} all-to-all(bf16[32,2,4,8,256]{4,2,0,1,3:T(4,128)(2,1)S(1)} %copy.37), channel_id=1, replica_groups=mesh['coil'=8,'frame'=4] {'coil'}, dimensions={3} | all-to-all | bytes 2097152 | tf_op jit(solution)/shard_map/all_to_all | solution.py:110
  318.4 17.3 %all_to_all.52 = bf16[256,2,4,1,256]{4,0,1,3,2:T(8,128)(2,1)S(1)} all-to-all(bf16[256,2,4,1,256]{4,0,1,3,2:T(8,128)(2,1)S(1)} %bitcast.75), channel_id=1, replica_groups=mesh['coil'=8,'frame'=4] {'frame'}, dimensions={2} | all-to-all | bytes 2097152 | tf_op jit(solution)/shard_map/all_to_all | solution.py:109
  336.9 5.1 multiply_reduce_fusion.1
  342.0 118.6 %all-gather.5.cloned.1.call-done = bf16[1024,2,1,2048]{3,0,1,2:T(8,128)(2,1)} async-done(((bf16[1024,2,1,256]{3,0,1,2:T(8,128)(2,1)}), bf16[1024,2,1,2048]{3,0,1,2:T(8,128)(2,1)}) %all-gather.5.cloned.1.call-update) | async-done | bytes 8388624 | tf_op jit(solution)/shard_map/all_gather | solution.py:121
  460.5 16.4 %copy.41 = bf16[1024,2,1,2048]{3,1,0,2:T(2,128)(2,1)} copy(bf16[1024,2,1,2048]{3,0,1,2:T(8,128)(2,1)} %all-gather.5.cloned.1.call-done) | data formatting | bytes 16777216 | tf_op jit(solution)/shard_map/all_gather | solution.py:121
  476.9 13.1 %reshape_squeeze.3 = bf16[2048,2048]{1,0:T(8,128)(2,1)} reshape(bf16[1024,2,1,2048]{3,1,0,2:T(2,128)(2,1)} %copy.41) | data formatting | bytes 16777216 | tf_op jit(solution)/shard_map/reshape;squeeze | solution.py:67
  495.0 6.2 pad_maximum_fusion
  501.2 16.4 %copy.42 = bf16[1024,2,2048]{2,1,0:T(2,128)(2,1)} copy(bf16[1024,2,2048]{2,0,1:T(8,128)(2,1)} %pad_maximum_fusion) | data formatting | bytes 16777216 | tf_op jit(solution)/shard_map/stack | solution.py:68
  517.6 13.1 %reshape.39 = bf16[2048,2048]{1,0:T(8,128)(2,1)} reshape(bf16[1024,2,2048]{2,1,0:T(2,128)(2,1)} %copy.42) | data formatting | bytes 16777216 | tf_op jit(solution)/shard_map/reshape | solution.py:68
  530.7 5.3 multiply_reduce_fusion
  536.5 43.1 %convolution_bitcast_fusion = f32[2048,4096]{1,0:T(8,128)} fusion(bf16[2048,2048]{1,0:T(8,128)(2,1)} %param.9, bf16[2048,2048]{1,0:T(8,128)(2,1)S(1)} %copy-done.1, bf16[2048,2048]{1,0:T(8,128)(2,1)} %reshape_squeeze.3), kind=kOutput, calls=%fused_computation.8 | convolution fusion | flops 34393292800 | bytes 58720256 | tf_op jit(solution)/shard_map/dot_general | solution.py:72
  579.6 18.3 %fusion.73 = (f32[2048]{0:T(1024)S(1)}, f32[2048,2048]{1,0:T(8,128)}) fusion(f32[2048]{0:T(1024)S(1)} %multiply_multiply_fusion, f32[2048]{0:T(1024)S(1)} %add_rsqrt_fusion, f32[2048,4096]{1,0:T(8,128)} %convolution_bitcast_fusion), kind=kLoop, calls=%fused_computation.97 | loop fusion | flops 25163776 | bytes 50356224 | tf_op jit(solution)/shard_map/reduce_max | solution.py:82
  597.8 18.8 %pmax.7 = f32[2048]{0:T(1024)S(1)} all-reduce(f32[2048]{0:T(1024)S(1)} %get-tuple-element.11), channel_id=1, replica_groups=mesh['coil'=8,'frame'=4] {'coil'}, use_global_device_ids=true, to_apply=%region_5.6 | all-reduce | flops 2048 | bytes 16384 | tf_op jit(solution)/shard_map/pmax | solution.py:128
  616.7 8.1 %fusion.11 = f32[2048]{0:T(1024)S(1)} fusion(f32[2048,2048]{1,0:T(8,128)} %get-tuple-element.12, f32[2048]{0:T(1024)S(1)} %get-tuple-element.11), kind=kLoop, calls=%fused_computation.21 | loop fusion | flops 8386560 | bytes 16793600 | tf_op jit(solution)/shard_map/reduce_sum | solution.py:84
  624.7 13.8 %fusion.23 = f32[6,2048]{1,0:T(8,128)S(1)} fusion(f32[6,2048]{1,0:T(8,128)S(1)} %copy-done, f32[2048,2048]{1,0:T(8,128)} %get-tuple-element.12, f32[2048]{0:T(1024)S(1)} %get-tuple-element.11, f32[2048]{0:T(1024)S(1)} %get-tuple-element.10), kind=kOutput, calls=%fused_computation.36 | convolution fusion | flops 306196480 | bytes 16891904 | tf_op jit(solution)/shard_map/dot_general | solution.py:85
  638.5 34.4 %all-reduce = (f32[6,2048]{1,0:T(8,128)S(1)}, f32[2048]{0:T(1024)S(1)}) all-reduce(f32[6,2048]{1,0:T(8,128)S(1)} %fusion.23, f32[2048]{0:T(1024)S(1)} %get-tuple-element.9), channel_id=1, replica_groups=mesh['coil'=8,'frame'=4] {'coil'}, use_global_device_ids=true, to_apply=%region_6.7 | all-reduce | flops 14336 | bytes 114688 | tf_op jit(solution)/shard_map/psum | solution.py:130
  (31 shorter events, 21.2 us)
Async XLA Ops:
  6.5 618.2 %copy-start = (f32[6,2048]{1,0:T(8,128)S(1)}, f32[6,2048]{1,0:T(8,128)}, u32[]{:S(2)}) copy-start(f32[6,2048]{1,0:T(8,128)} %param.10) | copy-start | bytes 147460
  6.5 12.8 %copy-start.3 = (s32[256,8]{0,1:T(8,128)S(1)}, s32[256,8]{0,1:T(8,128)}, u32[]{:S(2)}) copy-start(s32[256,8]{0,1:T(8,128)} %param.7) | copy-start | bytes 24580
  11.3 125.8 %all-to-all-start = ((bf16[4,256,8,256]{3,2,0,1:T(8,128)(2,1)}), bf16[4,256,8,256]{3,2,0,1:T(8,128)(2,1)}, u32[]{:S(2)}, u32[]{:S(2)}) async-start(bf16[4,256,8,256]{3,2,0,1:T(8,128)(2,1)} %copy.30), calls=%async_computation | async-start | bytes 8388608 | tf_op jit(solution)/shard_map/all_to_all | solution.py:98
  18.6 106.1 %all-gather.3.cloned.1.call-start = ((), (), s32[]{:S(2)}) async-start(), calls=%async_computation.3 | async-start | bytes 2359296 | tf_op jit(solution)/shard_map/all_gather | solution.py:104
  19.3 441.2 %all-gather.5.cloned.1.call-start = ((), (), s32[]{:S(2)}) async-start(), calls=%async_computation.4 | async-start | bytes 9437184 | tf_op jit(solution)/shard_map/all_gather | solution.py:121
  530.7 5.3 copy-start.2
  530.7 5.8 copy-start.1
Sparse Core Ops, SparseCore 0:
  21.5 103.1 all-gather.2
  337.0 123.5 all-gather.4
where the time goes:
time: 689 us; the launch traced here: 681 us
  waiting for transfers between devices  232 us (34%)
  matrix products  201 us (29%)
  blocking collectives  99.7 us (14%)
  local copies, waits for them, and re-layouts  77.6 us (11%)
  other arithmetic  49.2 us (7%)
  between operations  14 us (2%)
  starting transfers between devices  7.33 us (1%)
    all_gather x1, waiting for transfers between devices, body(): lax.all_gather(routed, 'coil', axis=3, tiled=True)[:, :, 0, :]  119 us
    all_gather x1, waiting for transfers between devices, body(): all_sens = lax.all_gather(sensitivity, 'coil', axis=0, tiled=True)  105 us
    dot_general x1, matrix products, coil_images(): jnp.einsum('fly,cflx->cfyx', sine_lines, real_part, precision=highest)  49.5 us
    dot_general x1, matrix products, match_stats(): inner = jnp.dot(dictionary, stacked, preferred_element_type=jnp.float32)  43.1 us
    psum x1, blocking collectives, body(): lax.psum((total_weight * factor, moments * factor[None, :]), 'coil')  34.4 us
    dot_general x1, matrix products, coil_images(): jnp.einsum('fly,cflx->cfyx', cos_lines, real_part, precision=highest)  31.2 us
    dot_general x1, matrix products, coil_images(): jnp.einsum('fly,cflx->cfyx', sine_lines, imag_part, precision=highest)  31.1 us
    dot_general x1, matrix products, coil_images(): jnp.einsum('fly,cflx->cfyx', cos_lines, imag_part, precision=highest)  31 us
  transfers between devices with their start and end apart: 3, of which 3 were waited for; matrix products, arithmetic and copies ran while one was open for 2% of the time, Pallas kernels for 0%

commit v1 on v0

v1 whole, which is shorter than its diff:
```python
import math

import jax
import jax.numpy as jnp
from jax import lax
from jax.sharding import PartitionSpec as P

NPE = 64
NRO = 128
ROWS = 64


def readout_table(length):
    position = jnp.arange(length, dtype=jnp.int32)
    angles = (position[:, None] * position[None, :] % length).astype(jnp.float32) * (
        2.0 * math.pi / length
    )
    cos_table = jnp.cos(angles)
    sine_table = jnp.sin(angles)
    upper_half = jnp.concatenate([cos_table, sine_table], axis=1)
    lower_half = jnp.concatenate([-sine_table, cos_table], axis=1)
    return jnp.concatenate([upper_half, lower_half], axis=0).astype(jnp.bfloat16)


def line_phases(line_index, row_count, length):
    row_index = jnp.arange(row_count, dtype=jnp.int32)
    angles = (line_index.T[:, :, None] * row_index[None, None, :] % length).astype(
        jnp.float32
    ) * (2.0 * math.pi / length)
    return (jnp.cos(angles), jnp.sin(angles))


def split(value):
    high = lax.reduce_precision(value, 8, 7)
    return high.astype(jnp.bfloat16), (value - high).astype(jnp.bfloat16)


def combined_images(samples, sens, cos_lines, sine_lines, table):
    coils, lines, frames, _ = samples.shape
    half = table.shape[1] // 2
    turned = samples.reshape(coils, lines * frames, samples.shape[3])
    spread = jnp.einsum(
        "cmk,krx->xrcm", turned, table.reshape(-1, 2, half), preferred_element_type=jnp.float32
    )
    g_high, g_low = split(spread.reshape(half, 2 * coils, lines * frames))
    left = jnp.concatenate([g_high, g_low, g_high], axis=1)
    sens_re = sens[:, 0].transpose(2, 0, 1)
    sens_im = sens[:, 1].transpose(2, 0, 1)
    from_re = jnp.concatenate([sens_re, -sens_im, sens_im, sens_re], axis=2)
    from_im = jnp.concatenate([sens_im, sens_re, -sens_re, sens_im], axis=2)
    s_high, s_low = split(jnp.concatenate([from_re, from_im], axis=1))
    right = jnp.concatenate([s_high, s_high, s_low], axis=1)
    sums = jnp.einsum("xkm,xkn->xmn", left, right, preferred_element_type=jnp.float32)
    rows = sens.shape[2]
    sums = sums.reshape(half, lines, frames, 4 * rows)
    cosine = jnp.concatenate([cos_lines, cos_lines], axis=2)
    sine = jnp.concatenate([sine_lines, sine_lines], axis=2)
    total = jnp.sum(
        cosine[None] * sums[..., : 2 * rows] + sine[None] * sums[..., 2 * rows :], axis=1
    ).astype(jnp.bfloat16)
    return total.reshape(half, frames, 2, rows).transpose(2, 1, 3, 0)


def column_orders(entries, frames, frame_groups, coil_groups):
    place = jnp.arange(entries, dtype=jnp.int32)
    run = place // (2 * frames)
    within = place % (2 * frames)
    part = within // frames
    frame = within % frames
    start = (run % frame_groups) * coil_groups + run // frame_groups
    base = start * (2 * frames) + 2 * frame
    source = place[:, None]
    direct = (source == (base + part)[None, :]).astype(jnp.bfloat16)
    sign = jnp.where(part == 0, -1.0, 1.0).astype(jnp.bfloat16)
    turned = (source == (base + 1 - part)[None, :]).astype(jnp.bfloat16) * sign[None, :]
    return direct, turned


def body(kspace, sampled_lines, sensitivity, dictionary, atom_params, concentration):
    frame_groups = lax.axis_size("frame")
    coil_groups = lax.axis_size("coil")
    frame_index = lax.axis_index("frame")
    coil_index = lax.axis_index("coil")
    voxel_total = sensitivity.shape[2]
    block_size = voxel_total // frame_groups
    local_frames = kspace.shape[1]
    few_frames = local_frames // coil_groups
    coils = kspace.shape[0] * coil_groups
    atoms, entries = dictionary.shape

    quarter = lax.dynamic_slice_in_dim(sensitivity, frame_index * block_size, block_size, 2)
    all_sens = lax.all_gather(quarter, ("coil", "frame"), axis=0)
    all_sens = (
        all_sens.reshape(coil_groups, frame_groups, kspace.shape[0], 2, block_size)
        .transpose(0, 2, 3, 1, 4)
        .reshape(coils, 2, ROWS, NRO)
    )
    lines_here = lax.dynamic_slice_in_dim(sampled_lines, coil_index * few_frames, few_frames, 0)
    cos_lines, sine_lines = line_phases(lines_here, ROWS, NPE)
    table = readout_table(NRO)

    pieces = PIECES if few_frames % (8 * PIECES) == 0 else 1
    step = few_frames // pieces
    grouped = kspace.reshape(kspace.shape[0], coil_groups, few_frames, *kspace.shape[2:])
    images = []
    for piece in range(pieces):
        part = slice(piece * step, (piece + 1) * step)
        sent = grouped[:, :, part].transpose(1, 0, 3, 2, 4)
        samples = lax.all_to_all(sent, "coil", split_axis=0, concat_axis=0, tiled=True)
        samples = samples.reshape(coils, *sent.shape[2:])
        images.append(
            combined_images(samples, all_sens, cos_lines[:, part], sine_lines[:, part], table)
        )
    image = jnp.concatenate(images, axis=1) if pieces > 1 else images[0]
    local = image.reshape(2 * few_frames, frame_groups, block_size).transpose(1, 0, 2)
    routed = lax.all_to_all(local, "frame", split_axis=0, concat_axis=0, tiled=True)
    routed = routed.reshape(frame_groups * 2 * few_frames, block_size)

    direct, turned = column_orders(entries, few_frames, frame_groups, coil_groups)
    straight = jnp.dot(dictionary, direct, preferred_element_type=jnp.float32)
    crossed = jnp.dot(dictionary, turned, preferred_element_type=jnp.float32)
    straight = straight.astype(jnp.bfloat16)
    crossed = crossed.astype(jnp.bfloat16)
    widened = dictionary.astype(jnp.float32)
    atom_scale = lax.rsqrt(jnp.mean(widened * widened, axis=1) + 1e-06)
    weighted = jnp.concatenate(
        [jnp.ones((1, atoms), jnp.float32), atom_params], axis=0
    )

    parts = PARTS if block_size % (128 * PARTS) == 0 else 1
    share = block_size // parts
    statistics = []
    for number in range(parts):
        span = slice(number * share, (number + 1) * share)
        fingerprints = lax.all_gather(
            routed[:, span], "coil", axis=0, tiled=True
        )
        inner_re = jnp.dot(straight, fingerprints, preferred_element_type=jnp.float32)
        inner_im = jnp.dot(crossed, fingerprints, preferred_element_type=jnp.float32)
        magnitude = jnp.sqrt(inner_re * inner_re + inner_im * inner_im)
        long = fingerprints.astype(jnp.float32)
        voxel_scale = lax.rsqrt(jnp.mean(long * long, axis=0) + 1e-06)
        logits = (
            magnitude
            * atom_scale[:, None]
            * (voxel_scale * concentration[span] / entries)[None, :]
        )
        peak = jnp.max(logits, axis=0)
        weights = jnp.exp(logits - peak[None, :])
        sums = jnp.dot(
            weighted, weights, precision=lax.Precision.HIGHEST,
            preferred_element_type=jnp.float32,
        )
        statistics.append(jnp.concatenate([peak[None], sums], axis=0))
    statistics = jnp.concatenate(statistics, axis=1) if parts > 1 else statistics[0]
    spread = jnp.broadcast_to(statistics[None], (coil_groups, *statistics.shape))
    everyone = lax.all_to_all(spread, "coil", split_axis=0, concat_axis=0, tiled=True)
    peaks = everyone[:, 0]
    factor = jnp.exp(peaks - jnp.max(peaks, axis=0)[None])
    sums = jnp.sum(everyone[:, 1:] * factor[:, None, :], axis=0)
    return sums[1:] / sums[:1]


PIECES = 2
PARTS = 1


def solution(mesh):
    in_specs = (
        P("coil", "frame", None, None),
        P("frame", None),
        P("coil", None, None),
        P("coil", None),
        P(None, "coil"),
        P("frame"),
    )
    out_specs = P(None, "frame")
    return jax.shard_map(body, mesh=mesh, in_specs=in_specs, out_specs=out_specs, check_vma=False)
```

time: 689 us -> 469 us (0.68)
  matrix products: 201 us -> 136 us
  blocking collectives: 99.7 us -> 34.8 us
  waiting for transfers between devices: 232 us -> 180 us
  local copies, waits for them, and re-layouts: 77.6 us -> 27.5 us
    all_gather x2, waiting for transfers between devices: 223 us -> 90.2 us  [the longest x1 76.7 us: body(): fingerprints = lax.all_gather(routed[:, span], 'coil', axis=0, tiled=True)]
    all_to_all x1 -> x2, waiting for transfers between devices: 8 us -> 89.9 us  [body(): lax.all_to_all(sent, 'coil', split_axis=0, concat_axis=0, tiled=True)]
    dot_general x7 -> x9, matrix products: 201 us -> 136 us  [the longest x1 30.9 us: body(): jnp.dot(crossed, fingerprints, preferred_element_type=jnp.float32)]
    psum x1 -> x0, blocking collectives: 34.4 us -> none  [body(): lax.psum((total_weight * factor, moments * factor[None, :]), 'coil')]
    another operation x5 -> x0, local copies, waits for them, and re-layouts: 30.3 us -> none  [the longest x1 16.4 us: match_stats(): jnp.stack([segment[:, 1], -segment[:, 0]], axis=1)]
    pmax x1 -> x0, blocking collectives: 18.8 us -> none  [body(): peak_global = lax.pmax(peak_score, 'coil')]
    reduce_max x1, other arithmetic: 18.3 us -> 0.06 us  [body(): factor = jnp.exp(peaks - jnp.max(peaks, axis=0)[None])]
    all_gather x1 -> x0, local copies, waits for them, and re-layouts: 16.4 us -> none  [body(): lax.all_gather(routed, 'coil', axis=3, tiled=True)[:, :, 0, :]]
  transfers between devices with their start and end apart: 3 -> 4, of which waited for: 3 -> 4; matrix products, arithmetic and copies ran while one was open for 2% -> 15% of each run, Pallas kernels for 0% -> 0%
where the time goes in v1:
time: 469 us; the launch traced here: 460 us
  waiting for transfers between devices  180 us (38%)
  matrix products  136 us (29%)
  other arithmetic  55.2 us (12%)
  blocking collectives  34.8 us (7%)
  local copies, waits for them, and re-layouts  27.5 us (6%)
  between operations  14.2 us (3%)
  starting transfers between devices  11.7 us (2%)
    all_to_all x2, waiting for transfers between devices, body(): lax.all_to_all(sent, 'coil', split_axis=0, concat_axis=0, tiled=True)  89.9 us
    all_gather x1, waiting for transfers between devices, body(): fingerprints = lax.all_gather(routed[:, span], 'coil', axis=0, tiled=True)  76.7 us
    dot_general x1, matrix products, body(): jnp.dot(crossed, fingerprints, preferred_element_type=jnp.float32)  30.9 us
    dot_general x2, matrix products, combined_images(): jnp.einsum('xkm,xkn->xmn', left, right, preferred_element_type=jnp.float32)  26.2 us
    reduce_sum x2, other arithmetic, combined_images(): jnp.sum(cosine[None] * sums[..., :2 * rows] + sine[None] * sums[..., 2 *...  24.2 us
    dot_general x1, matrix products, body(): jnp.dot(straight, fingerprints, preferred_element_type=jnp.float32)  22.9 us
    dot_general x1, matrix products, body(): straight = jnp.dot(dictionary, direct, preferred_element_type=jnp.float32)  21.8 us
    dot_general x1, matrix products, body(): crossed = jnp.dot(dictionary, turned, preferred_element_type=jnp.float32)  20.1 us
  transfers between devices with their start and end apart: 4, of which 4 were waited for; matrix products, arithmetic and copies ran while one was open for 15% of the time, Pallas kernels for 0%

profile of v1, /device:TPU:0, one launch (start us, length us, event | category | flops | bytes accessed | tf_op | source)
XLA Modules:
  0.0 459.9 jit_solution(272588094507078487)
XLA Ops:
  6.5 4.1 fusion.96
  12.6 7.3 %all-to-all-start.1 = ((bf16[8,4,8,16,256]{4,3,2,1,0:T(8,128)(2,1)}), bf16[8,4,8,16,256]{4,3,2,1,0:T(8,128)(2,1)S(1)}, u32[]{:S(2)}, u32[]{:S(2)}) async-start(bf16[8,4,8,16,256]{4,3,2,1,0:T(8,128)(2,1)} %bitcast.82), calls=%async_computation.1 | async-start | bytes 4194304 | tf_op jit(solution)/shard_map/all_to_all | solution.py:109
  23.4 44.7 %all-to-all-done.1 = bf16[8,4,8,16,256]{4,3,2,1,0:T(8,128)(2,1)S(1)} async-done(((bf16[8,4,8,16,256]{4,3,2,1,0:T(8,128)(2,1)}), bf16[8,4,8,16,256]{4,3,2,1,0:T(8,128)(2,1)S(1)}, u32[]{:S(2)}, u32[]{:S(2)}) %all-to-all-start.1) | async-done | bytes 2097184 | tf_op jit(solution)/shard_map/all_to_all | solution.py:109
  68.1 4.3 all-to-all-start
  77.6 45.3 %all-to-all-done = bf16[8,4,8,16,256]{4,3,2,1,0:T(8,128)(2,1)} async-done(((bf16[8,4,8,16,256]{4,3,2,1,0:T(8,128)(2,1)}), bf16[8,4,8,16,256]{4,3,2,1,0:T(8,128)(2,1)}, u32[]{:S(2)}, u32[]{:S(2)}) %all-to-all-start) | async-done | bytes 2097184 | tf_op jit(solution)/shard_map/all_to_all | solution.py:109
  125.7 4.7 %fusion.37 = (bf16[128,64,128]{2,1,0:T(8,128)(2,1)}, bf16[128,64,128]{2,1,0:T(8,128)(2,1)}) fusion(f32[128,64,128]{2,0,1:T(8,128)S(1)} %bitcast.76), kind=kLoop, calls=%fused_computation.48 | loop fusion | flops 4194304 | bytes 8388608 | tf_op jit(solution)/shard_map/convert_element_type | solution.py:35
  130.4 4.7 %fusion.36 = (bf16[128,64,128]{2,1,0:T(8,128)(2,1)}, bf16[128,64,128]{2,1,0:T(8,128)(2,1)}) fusion(f32[128,64,128]{2,0,1:T(8,128)S(1)} %bitcast.77), kind=kLoop, calls=%fused_computation.47 | loop fusion | flops 4194304 | bytes 8388608 | tf_op jit(solution)/shard_map/convert_element_type | solution.py:35
  135.1 13.5 %all-gather.6.cloned.1.call-done = f32[128,2,2048]{2,1,0:T(2,128)} async-done(((f32[4,2,2048]{2,1,0:T(2,128)}), f32[128,2,2048]{2,1,0:T(2,128)}) %all-gather.6.cloned.1.call-update) | async-done | bytes 2097168 | tf_op jit(solution)/shard_map/all_gather | solution.py:92
  148.6 4.7 %copy.85 = f32[8,4,4,2,2048]{4,1,3,2,0:T(4,128)} copy(f32[8,4,4,2,2048]{4,3,2,1,0:T(2,128)} %bitcast.87) | data formatting | bytes 4194304 | tf_op jit(solution)/shard_map/reshape | solution.py:94
  165.2 6.4 %reduce-precision_convert_fusion = (bf16[128,64,256]{2,1,0:T(8,128)(2,1)S(1)}, bf16[128,64,256]{2,1,0:T(8,128)(2,1)}) fusion(f32[128,32,64]{2,1,0:T(8,128)S(1)} %bitcast.72, f32[128,32,64]{2,1,0:T(8,128)S(1)} %get-tuple-element.25, f32[128,32,64]{2,1,0:T(8,128)S(1)} %bitcast.73, f32[128,32,64]{2,1,0:T(8,128)S(1)} %get-tuple-element.26), kind=kLoop, calls=%fused_computation.12 | loop fusion | flops 23068672 | bytes 12582912 | tf_op jit(solution)/shard_map/convert_element_type | solution.py:35
  171.5 10.9 %fusion.24 = f32[128,128,256]{2,1,0:T(8,128)} fusion(bf16[128,64,256]{2,1,0:T(8,128)(2,1)} %get-tuple-element.6, bf16[128,64,256]{2,1,0:T(8,128)(2,1)S(1)} %get-tuple-element.5, bf16[128,64,128]{2,1,0:T(8,128)(2,1)} %get-tuple-element.12, bf16[128,64,128]{2,1,0:T(8,128)(2,1)S(1)} %copy-done.7), kind=kOutput, calls=%fused_computation.31 | convolution fusion | flops 1667235840 | bytes 29360128 | tf_op jit(solution)/shard_map/xkm,xkn->xmn/dot_general | solution.py:53
  182.4 7.5 %fusion.11 = bf16[128,16,128]{2,1,0:T(8,128)(2,1)S(1)} fusion(f32[128,8,16,256]{3,2,1,0:T(8,128)} %bitcast.75, f32[8,16,128]{2,1,0:T(8,128)S(1)} %pad_maximum_fusion.7, f32[8,16,128]{2,1,0:T(8,128)S(1)} %pad_maximum_fusion.6), kind=kLoop, calls=%fused_computation.18 | loop fusion | flops 8126464 | bytes 17432576 | tf_op jit(solution)/shard_map/reduce_sum | solution.py:58
  190.4 15.3 %fusion.25 = f32[128,128,256]{2,1,0:T(8,128)} fusion(bf16[128,64,256]{2,1,0:T(8,128)(2,1)} %get-tuple-element.6, bf16[128,64,256]{2,1,0:T(8,128)(2,1)} %copy-done.5, bf16[128,64,128]{2,1,0:T(8,128)(2,1)} %get-tuple-element.8, bf16[128,64,128]{2,1,0:T(8,128)(2,1)S(1)} %copy-done.6), kind=kOutput, calls=%fused_computation.32 | convolution fusion | flops 1667235840 | bytes 29360128 | tf_op jit(solution)/shard_map/xkm,xkn->xmn/dot_general | solution.py:53
  205.7 16.6 %fusion.13 = bf16[128,16,128]{2,1,0:T(8,128)(2,1)S(1)} fusion(f32[128,8,16,256]{3,2,1,0:T(8,128)} %bitcast.74, f32[8,16,128]{2,1,0:T(8,128)S(1)} %pad_maximum_fusion.5, f32[8,16,128]{2,1,0:T(8,128)S(1)} %pad_maximum_fusion.4), kind=kLoop, calls=%fused_computation.22 | loop fusion | flops 8126464 | bytes 17432576 | tf_op jit(solution)/shard_map/reduce_sum | solution.py:58
  223.9 17.6 %all_to_all.20 = bf16[4,64,2048]{2,1,0:T(8,128)(2,1)} all-to-all(bf16[4,64,2048]{2,1,0:T(8,128)(2,1)S(1)} %copy.62), channel_id=1, replica_groups=mesh['coil'=8,'frame'=4] {'frame'}, dimensions={0} | all-to-all | bytes 2097152 | tf_op jit(solution)/shard_map/all_to_all | solution.py:116
  241.6 5.2 %multiply_reduce_fusion.1 = f32[2048]{0:T(1024)S(1)} fusion(bf16[2048,2048]{1,0:T(8,128)(2,1)} %param.9), kind=kLoop, calls=%fused_computation.5 | loop fusion | flops 12580864 | bytes 8396800 | tf_op jit(solution)/shard_map/reduce_sum | solution.py:125
  246.8 21.8 %fusion.123 = bf16[2048,2048]{1,0:T(8,128)(2,1)} fusion(bf16[2048,2048]{1,0:T(8,128)(2,1)} %param.9, s32[2048]{0:T(1024)S(1)} %fusion.88), kind=kOutput, calls=%fused_computation.29.clone.1 | convolution fusion | flops 17192452096 | bytes 16785408 | tf_op jit(solution)/shard_map/dot_general | solution.py:120
  268.7 20.1 %fusion.15.clone.4 = bf16[2048,2048]{1,0:T(8,128)(2,1)} fusion(bf16[2048,2048]{1,0:T(8,128)(2,1)S(1)} %bitcast.80, s32[2048]{0:T(1024)S(1)} %add_subtract_fusion, bf16[2048]{0:T(1024)(128)(2,1)S(1)} %get-tuple-element.30), kind=kOutput, calls=%fused_computation.26.clone.clone.clone.1 | convolution fusion | flops 17192452096 | bytes 16789504 | tf_op jit(solution)/shard_map/dot_general | solution.py:121
  288.7 76.7 %all-gather.4.cloned.1.call-done = bf16[2048,2048]{1,0:T(8,128)(2,1)} async-done(((bf16[256,2048]{1,0:T(8,128)(2,1)}), bf16[2048,2048]{1,0:T(8,128)(2,1)}) %all-gather.4.cloned.1.call-update) | async-done | bytes 8388624 | tf_op jit(solution)/shard_map/all_gather | solution.py:135
  365.4 5.3 %multiply_reduce_fusion = f32[2048]{0:T(1024)S(1)} fusion(bf16[2048,2048]{1,0:T(8,128)(2,1)} %all-gather.4.cloned.1.call-done), kind=kLoop, calls=%fused_computation.3 | loop fusion | flops 12580864 | bytes 8396800 | tf_op jit(solution)/shard_map/reduce_sum | solution.py:142
  371.2 22.9 %fusion.17 = f32[2048,2048]{1,0:T(8,128)} fusion(bf16[2048,2048]{1,0:T(8,128)(2,1)S(1)} %copy-done.4, bf16[2048,2048]{1,0:T(8,128)(2,1)} %fusion.123), kind=kOutput, calls=%fused_computation.28 | convolution fusion | flops 17179869184 | bytes 33554432 | tf_op jit(solution)/shard_map/dot_general | solution.py:138
  394.0 30.9 %fusion.100 = (f32[2048]{0:T(1024)S(1)}, f32[2048,2048]{1,0:T(8,128)S(1)}) fusion(f32[2048]{0:T(1024)S(1)} %multiply_multiply_fusion.1, f32[2048]{0:T(1024)S(1)} %get-tuple-element.29, bf16[2048,2048]{1,0:T(8,128)(2,1)} %all-gather.4.cloned.1.call-done, f32[2048,2048]{1,0:T(8,128)} %fusion.17, bf16[2048,2048]{1,0:T(8,128)(2,1)} %fusion.15.clone.4), kind=kOutput, calls=%fused_computation.151 | convolution fusion | flops 17205032960 | bytes 50356224 | tf_op jit(solution)/shard_map/dot_general | solution.py:139
  425.0 9.4 %fusion = f32[7,2048]{1,0:T(8,128)S(1)} fusion(f32[2048,2048]{1,0:T(8,128)S(1)} %get-tuple-element.22, f32[2048]{0:T(1024)S(1)} %get-tuple-element.21, f32[6,2048]{1,0:T(8,128)S(1)} %copy-done.8), kind=kOutput, calls=%fused_computation | convolution fusion | flops 356515840 | bytes 16891904 | tf_op jit(solution)/shard_map/dot_general | solution.py:150
  434.5 17.2 %all_to_all.21 = f32[8,8,2048]{2,1,0:T(8,128)S(1)} all-to-all(f32[8,8,2048]{2,1,0:T(8,128)S(1)} %broadcast_in_dim.15), channel_id=1, replica_groups=mesh['coil'=8,'frame'=4] {'coil'}, dimensions={0} | all-to-all | bytes 1048576 | tf_op jit(solution)/shard_map/all_to_all | solution.py:157
  (68 shorter events, 28.7 us)
Async XLA Ops:
  6.5 66.0 %copy-start = (f32[4,2,8192]{2,1,0:T(2,128)S(1)}, f32[4,2,8192]{2,1,0:T(2,128)}, u32[]{:S(2)}) copy-start(f32[4,2,8192]{2,1,0:T(2,128)} %param.8) | copy-start | bytes 786436
  10.6 62.6 %copy-start.10 = (s32[256,8]{0,1:T(8,128)S(1)}, s32[256,8]{0,1:T(8,128)}, u32[]{:S(2)}) copy-start(s32[256,8]{0,1:T(8,128)} %param.7) | copy-start | bytes 24580
  12.6 55.5 %all-to-all-start.1 = ((bf16[8,4,8,16,256]{4,3,2,1,0:T(8,128)(2,1)}), bf16[8,4,8,16,256]{4,3,2,1,0:T(8,128)(2,1)S(1)}, u32[]{:S(2)}, u32[]{:S(2)}) async-start(bf16[8,4,8,16,256]{4,3,2,1,0:T(8,128)(2,1)} %bitcast.82), calls=%async_computation.1 | async-start | bytes 4194304 | tf_op jit(solution)/shard_map/all_to_all | solution.py:109
  68.1 54.8 %all-to-all-start = ((bf16[8,4,8,16,256]{4,3,2,1,0:T(8,128)(2,1)}), bf16[8,4,8,16,256]{4,3,2,1,0:T(8,128)(2,1)}, u32[]{:S(2)}, u32[]{:S(2)}) async-start(bf16[8,4,8,16,256]{4,3,2,1,0:T(8,128)(2,1)} %bitcast.81), calls=%async_computation | async-start | bytes 4194304 | tf_op jit(solution)/shard_map/all_to_all | solution.py:109
  72.5 76.1 %all-gather.6.cloned.1.call-start = ((), (), s32[]{:S(2)}) async-start(), calls=%async_computation.5 | async-start | bytes 2162688 | tf_op jit(solution)/shard_map/all_gather | solution.py:92
  73.2 292.2 %all-gather.4.cloned.1.call-start = ((), (), s32[]{:S(2)}) async-start(), calls=%async_computation.4 | async-start | bytes 9437184 | tf_op jit(solution)/shard_map/all_gather | solution.py:135
  122.9 2.8 copy-start.3
  162.9 2.2 copy-start.2
  165.2 6.4 %copy-start.7 = (bf16[128,64,128]{2,1,0:T(8,128)(2,1)S(1)}, bf16[128,64,128]{2,1,0:T(8,128)(2,1)}, u32[]{:S(2)}) copy-start(bf16[128,64,128]{2,1,0:T(8,128)(2,1)} %get-tuple-element.11) | copy-start | bytes 6291460
  171.5 10.9 %copy-start.5 = (bf16[128,64,256]{2,1,0:T(8,128)(2,1)}, bf16[128,64,256]{2,1,0:T(8,128)(2,1)S(1)}, u32[]{:S(2)}) copy-start(bf16[128,64,256]{2,1,0:T(8,128)(2,1)S(1)} %get-tuple-element.5) | copy-start | bytes 12582916
  182.4 8.0 %copy-start.6 = (bf16[128,64,128]{2,1,0:T(8,128)(2,1)S(1)}, bf16[128,64,128]{2,1,0:T(8,128)(2,1)}, u32[]{:S(2)}) copy-start(bf16[128,64,128]{2,1,0:T(8,128)(2,1)} %get-tuple-element.7) | copy-start | bytes 6291460
  241.6 27.1 %slice-start = ((s8[8388608]{0:T(1024)(128)(4,1)}), s8[4194304]{0:T(1024)(128)(4,1)S(1)}, s32[]{:S(2)}) async-start(s8[8388608]{0:T(1024)(128)(4,1)} %bitcast.79), calls=%async_computation.6 | async-start | bytes 8388608
  246.8 21.8 %slice-start.1 = ((s8[8388608]{0:T(1024)(128)(4,1)}), s8[4194304]{0:T(1024)(128)(4,1)S(1)}, s32[]{:S(2)}) async-start(s8[8388608]{0:T(1024)(128)(4,1)} %bitcast.79), calls=%async_computation.7 | async-start | bytes 8388608
  288.7 82.0 %copy-start.9 = (f32[2048]{0:T(1024)S(1)}, f32[2048]{0:T(1024)}, u32[]{:S(2)}) copy-start(f32[2048]{0:T(1024)} %param.11) | copy-start | bytes 24580
  365.4 5.8 %copy-start.4 = (bf16[2048,2048]{1,0:T(8,128)(2,1)S(1)}, bf16[2048,2048]{1,0:T(8,128)(2,1)}, u32[]{:S(2)}) copy-start(bf16[2048,2048]{1,0:T(8,128)(2,1)} %all-gather.4.cloned.1.call-done) | copy-start | bytes 25165828
  394.0 30.9 %copy-start.8 = (f32[6,2048]{1,0:T(8,128)S(1)}, f32[6,2048]{1,0:T(8,128)}, u32[]{:S(2)}) copy-start(f32[6,2048]{1,0:T(8,128)} %param.10) | copy-start | bytes 147460
  425.0 27.7 %copy-start.1 = (f32[4,2,8192]{2,1,0:T(2,128)S(1)}, f32[4,2,8192]{2,1,0:T(2,128)}, u32[]{:S(2)}) copy-start(f32[4,2,8192]{2,1,0:T(2,128)} %param.8) | copy-start | bytes 786436
Sparse Core Ops, SparseCore 0:
  76.2 72.3 all-gather.5
  241.6 123.7 all-gather.3
